TPU v7x, 128 devices: a whole 4x4x4 slice. The times are simulated.
128 devices in a mesh: gx: 16 (over y_lo, z, core), gy: 8 (over y_hi, x).
Axes of the slice: x: 4, y: 4 (y_hi: 2, y_lo: 2; y = y_hi * 2 + y_lo), z: 4, core: 2. Of those that a mesh axis runs over, the one named last changes fastest.
Arguments:
- e_field: float32 [3, 64, 64, 1024], P(None, None, 'gx', 'gy'), may hold values from -6 to 6
- h_field: float32 [3, 64, 64, 1024], P(None, None, 'gx', 'gy'), may hold values from -6 to 6
- drude_current: float32 [3, 64, 64, 1024], P(None, None, 'gx', 'gy'), may hold values from -6 to 6
- lorentz_polar: float32 [3, 64, 64, 1024], P(None, None, 'gx', 'gy'), may hold values from -6 to 6
- lorentz_rate: float32 [3, 64, 64, 1024], P(None, None, 'gx', 'gy'), may hold values from -6 to 6
- permittivity: float32 [64, 64, 1024], P(None, 'gx', 'gy'), may hold values from 1 to 6
- material: int32 [64, 64, 1024], P(None, 'gx', 'gy'), may hold values from 0 to 2
- absorber: int32 [64, 64, 1024], P(None, 'gx', 'gy'), may hold values from 0 to 3
Outputs:
- e_out: float32 [3, 64, 64, 1024], P(None, None, 'gx', 'gy')
- h_out: float32 [3, 64, 64, 1024], P(None, None, 'gx', 'gy')
All inputs are finite; a program needn't handle non-finite values.
Results may differ from a plain program's by a relative error of at most 0.00002.
Values sent between devices are 32-bit elements; how exact they have to be, the bound alone decides.
A program may use at most 64 MiB of HBM per device.

v0:
```python
import contextlib

import jax
import jax.numpy as jnp
from jax import lax
from jax.experimental import pallas as pl
from jax.experimental.pallas import tpu as pltpu
from jax.sharding import PartitionSpec as P

STEPS = 14
BLOCKS = 4
MESH = pl.DeviceIdType.MESH
NAMED = False
F32 = jnp.float32

TILES = 10
TILE = 16
COMP = 12 * TILE
ROWS = 80
OWN = 2
CROSS = 8
ZERO_H = 9
FREE = 10
ZERO_E = 14
PLANES = 15

C_J = 0.975 / 1.025
C_E = 2.0 * (1.125 / 1.025)

SLOTS = ["perm", "mat", "abs", "e0", "e1", "e2", "h0", "h1", "h2", "j0", "j1", "j2", "p0", "p1", "p2", "q0", "q1", "q2"]
GROUPS = 5


def scope(name):
    return jax.named_scope(name) if NAMED else contextlib.nullcontext()


def towards(axis, step):
    count = lax.axis_size(axis)
    return {axis: lax.rem(lax.axis_index(axis) + step + count, count)}


def lanes(rows=8):
    return lax.broadcasted_iota(jnp.int32, (rows, 128), 1)


def loop(low, high, body):
    lax.fori_loop(low, high, lambda i, carry: (body(i), carry)[1], 0)


def at(c, t, shift=0):
    return pl.ds(COMP * c + TILE * (t + 1) + shift, 8)


def packed(c, t):
    return pl.ds(ROWS * c + 8 * t, 8)


class Tiles:
    def __init__(self, ref, plane):
        self.ref, self.plane, self.held = ref, plane, {}

    def __call__(self, c, t):
        if (c, t) not in self.held:
            self.held[c, t] = self.ref[self.plane, at(c, t)]
        return self.held[c, t]


def pipelined(load, work):
    loaded = load(0)
    for t in range(TILES):
        later = load(t + 1) if t + 1 < TILES else None
        work(t, loaded)
        loaded = later


def h_pass(e, h, ah, bh, src, nxt, dst, cell):
    tile = Tiles(e, src)

    def load(t):
        here = pl.ds(8 * t, 8)
        return (
            [tile(c, t) for c in range(3)],
            tile(0, t + 1), tile(2, t + 1),
            e[src, at(0, t, 1)], e[src, at(1, t, 1)],
            e[nxt, at(1, t)], e[nxt, at(2, t)],
            [h[src, at(c, t)] for c in range(3)],
            ah[cell, here], bh[cell, here],
        )

    def work(t, loaded):
        (ex, ey, ez), ex_y, ez_y, ex_z, ey_z, ey_x, ez_x, (hx, hy, hz), a, b = loaded
        h[dst, at(0, t)] = a * hx - b * ((ez_y - ez) - (ey_z - ey))
        h[dst, at(1, t)] = a * hy - b * ((ex_z - ex) - (ez_x - ez))
        h[dst, at(2, t)] = a * hz - b * ((ey_x - ey) - (ex_y - ex))

    pipelined(load, work)


def e_pass(e, h, j, p, q, ae, be, bm, src, mag, prv, dst, cell):
    tile = Tiles(h, mag)

    def load(t):
        here = pl.ds(8 * t, 8)
        media = [(e[src, at(c, t)], j[src, packed(c, t)], p[src, packed(c, t)], q[src, packed(c, t)]) for c in range(3)]
        return (
            media,
            [tile(c, t) for c in range(3)],
            tile(0, t - 1), tile(2, t - 1),
            h[mag, at(0, t, -1)], h[mag, at(1, t, -1)],
            h[prv, at(1, t)], h[prv, at(2, t)],
            ae[cell, here], be[cell, here], bm[cell, here],
        )

    def work(t, loaded):
        media, (hx, hy, hz), hx_y, hz_y, hx_z, hy_z, hy_x, hz_x, a, b, m = loaded
        curl = (
            (hz - hz_y) - (hy - hy_z),
            (hx - hx_z) - (hz - hz_x),
            (hy - hy_x) - (hx - hx_y),
        )
        for c in range(3):
            ec, jc, pc, qc = media[c]
            jc = C_J * jc + C_E * ec
            qc = 0.9 * qc + (ec - pc)
            pc = pc + 0.25 * qc
            j[dst, packed(c, t)] = jc
            q[dst, packed(c, t)] = qc
            p[dst, packed(c, t)] = pc
            e[dst, at(c, t)] = a * ec + (b * curl[c] - m * (jc + qc))

    pipelined(load, work)


def edges_e(e, plane):
    tiles = [e[plane, at(c, 0)] for c in (0, 2)]
    first = e[plane, pl.ds(0, 24, stride=TILE)]
    tiles = [pltpu.roll(tile, 127, 1) for tile in tiles]
    first = jnp.where(lanes(24) < 112, pltpu.roll(first, 112, 1), 0.0)

    def store():
        e[plane, at(0, TILES)], e[plane, at(2, TILES)] = tiles
        e[plane, pl.ds(8, 24, stride=TILE)] = first

    return store


def edges_h(h, plane):
    tiles = [h[plane, at(c, TILES - 1)] for c in (0, 2)]
    last = h[plane, pl.ds(TILE + 7, 24, stride=TILE)]
    tiles = [pltpu.roll(tile, 1, 1) for tile in tiles]
    last = jnp.where(lanes(24) < 16, 0.0, pltpu.roll(last, 16, 1))

    def store():
        h[plane, at(0, -1)], h[plane, at(2, -1)] = tiles
        h[plane, pl.ds(TILE - 1, 24, stride=TILE)] = last

    return store


def kernel(
    e_in, h_in, j_in, p_in, q_in, perm_in, mat_in, abs_in, e_out, h_out,
    stage, ints, turned, raw, e, h, j, p, q, ah, bh, ae, be, bm,
    send_e, send_h, recv_e, recv_h, in_sem, y_sem, x_sem, se_sem, re_sem, sh_sem, rh_sem,
):
    barrier = pltpu.get_barrier_semaphore()
    for axis in ("gx", "gy"):
        for step in (-1, 1):
            pl.semaphore_signal(barrier, inc=1, device_id=towards(axis, step), device_id_type=MESH)

    fields = (e_in, h_in, j_in, p_in, q_in)
    loads = {
        "perm": pltpu.make_async_copy(perm_in, stage.at[0], in_sem.at[5]),
        "mat": pltpu.make_async_copy(mat_in, ints.at[0], in_sem.at[6]),
        "abs": pltpu.make_async_copy(abs_in, ints.at[1], in_sem.at[7]),
    }
    for i, f in enumerate(fields):
        loads["ehjpq"[i]] = pltpu.make_async_copy(f, stage.at[pl.ds(3 + 3 * i, 3)], in_sem.at[i])
    for load in loads.values():
        load.start()

    def clear(planes, refs):
        for ref in refs:
            size = ref.shape[1] // 6

            def body(i):
                for plane in planes:
                    for k in range(size // 8):
                        ref[plane, pl.ds(pl.multiple_of(size * i + 8 * k, 8), 8)] = jnp.zeros((8, 128), F32)

            loop(0, 6, body)

    clear((ZERO_E,), (e,))
    clear((ZERO_H,), (h,))

    def turn(g):
        def body(zb):
            rows = []
            for s in range(4):
                slot = 4 * g + s
                for x in range(4):
                    here = pl.ds(x, 8, stride=4)
                    if slot in (1, 2):
                        rows.append(ints[slot - 1, zb, here].astype(F32))
                    else:
                        rows.append(stage[min(slot, 17), zb, here])
            turned[g, zb, pl.ds(16, 128)] = jnp.transpose(jnp.concatenate(rows, 0))

        loop(0, 8, body)

    def columns(g, step):
        source, target = (pl.ds(16, 16), pl.ds(144, 16)) if step < 0 else (pl.ds(128, 16), pl.ds(0, 16))
        k = 2 * g + (step + 1) // 2
        return pltpu.make_async_remote_copy(
            src_ref=turned.at[g, :, source], dst_ref=turned.at[g, :, target],
            send_sem=y_sem.at[0, k], recv_sem=y_sem.at[1, k],
            device_id=towards("gy", step), device_id_type=MESH,
        )

    waited = set()
    for g in range(GROUPS):
        with scope("turn"):
            for name in SLOTS[4 * g : 4 * g + 4]:
                name = name if name in loads else name[0]
                if name not in waited:
                    waited.add(name)
                    loads[name].wait()
            turn(g)
        if g == 0:
            with scope("barrier"):
                pl.semaphore_wait(barrier, 4)
        for step in (-1, 1):
            columns(g, step).start()

    state = {"e": e, "h": h, "j": j, "p": p, "q": q}

    def build(g):
        def body(t):
            rows = [turned[g, zb, pl.ds(t, 16, stride=10)] for zb in range(8)]
            whole = jnp.transpose(jnp.concatenate(rows, 0))
            for s, name in enumerate(SLOTS[4 * g : 4 * g + 4]):
                for x in range(4):
                    part = whole[32 * s + 8 * x : 32 * s + 8 * x + 8]
                    if 4 * g + s < 3:
                        raw[OWN + x, 4 * g + s, pl.ds(pl.multiple_of(8 * t, 8), 8)] = part
                        continue
                    c = int(name[1])
                    if name[0] in "eh":
                        row = COMP * c + TILE * (t + 1)
                    else:
                        row = ROWS * c + 8 * t
                    if name[0] in "jq":
                        part = part * 2.0
                    state[name[0]][OWN + x, pl.ds(pl.multiple_of(row, 8), 8)] = part

        loop(0, TILES, body)

    def layers(step):
        source, target = (OWN, OWN + 4) if step < 0 else (OWN + 2, OWN - 2)
        k = (step + 1) // 2
        return pltpu.make_async_remote_copy(
            src_ref=raw.at[pl.ds(source, 2)], dst_ref=raw.at[pl.ds(target, 2)],
            send_sem=x_sem.at[0, k], recv_sem=x_sem.at[1, k],
            device_id=towards("gx", step), device_id_type=MESH,
        )

    def coefficients(plane):
        for t in range(TILES):
            here = pl.ds(8 * t, 8)
            perm, mat, absorb = (raw[plane, i, here] for i in range(3))
            s = 0.1 * absorb
            eff = jnp.where(mat == 0.0, 1.0, perm)
            r = 1.0 / (1.0 + s)
            ah[plane, here] = (1.0 - s) * r
            bh[plane, here] = 0.5 * r
            se = s / eff
            r = 1.0 / (1.0 + se)
            ae[plane, here] = (1.0 - se) * r
            b = 0.5 * r / eff
            be[plane, here] = b
            bm[plane, here] = jnp.where(mat == 2.0, 0.5 * b, 0.0)

    for g in range(GROUPS):
        with scope("ghosts"):
            for step in (-1, 1):
                columns(g, step).wait()
        with scope("build"):
            build(g)
        if g == 0:
            for step in (-1, 1):
                layers(step).start()
            loop(OWN, OWN + 4, coefficients)
        if g == 1:
            loop(OWN, OWN + 4, lambda x: edges_e(e, x)())

    def trace_e(step):
        return pltpu.make_async_remote_copy(
            src_ref=send_e.at[step], dst_ref=recv_e.at[step],
            send_sem=se_sem.at[step], recv_sem=re_sem.at[step],
            device_id=towards("gx", -1), device_id_type=MESH,
        )

    def trace_h(step):
        return pltpu.make_async_remote_copy(
            src_ref=send_h.at[step], dst_ref=recv_h.at[step],
            send_sem=sh_sem.at[step], recv_sem=rh_sem.at[step],
            device_id=towards("gx", 1), device_id_type=MESH,
        )

    def give(ref, plane, out, step):
        for c in range(2):
            for t in range(TILES):
                out[step, c, pl.ds(8 * t, 8)] = ref[plane, at(1 + c, t)]

    def take(ref, plane, trace, step):
        for c in range(2):
            for t in range(TILES):
                ref[CROSS, at(1 + c, t)] = ref[plane, at(1 + c, t)] + trace[step, c, pl.ds(8 * t, 8)]

    def block(b, carry):
        size = 4 - b // 2
        start = 4 * b - b // 3

        def free_h(x, base):
            nxt = base + x + 1 + (x // 3) * (ZERO_E - base - 4)
            h_pass(e, h, ah, bh, base + x, nxt, FREE + x, OWN + x)

        def free_e(x, base):
            e_pass(e, h, j, p, q, ae, be, bm, base + x, FREE + x, FREE + x - 1, FREE + x, OWN + x)

        def give_e(plane, step):
            give(e, plane, send_e, step)
            trace_e(step).start()

        def give_h(step):
            give(h, FREE + 3, send_h, step)
            trace_h(step).start()

        def free(i):
            base = OWN + ((i + 3) // 4) * (FREE - OWN)
            last = (i + 2) // size
            give_e(base, start + i)
            store = edges_e(e, base + 2)
            free_h(3, base)
            store()
            give_h(start + i)

            def more_h(x):
                store = edges_h(h, FREE + x - 1 + 4 * (1 - (x + 2) // 3))
                free_h(x, base)
                store()

            loop(0, 3, more_h)
            store = edges_h(h, FREE + 2)
            free_e(3, base)
            store()

            def more_e(x):
                store = edges_e(e, FREE + x - 1 + 4 * (1 - (x + 2) // 3))
                free_e(x, base)
                store()

            loop(0, 3 - 2 * last, more_e)

        with scope("free"):
            loop(0, size - 1, free)
            give_e(FREE, start + size - 1)
            free_h(3, FREE)
            give_h(start + size - 1)

        with scope("clear"):
            clear((0, 1, 6, 7), (e, h, j, p, q))

        def ghost_coefficients(i):
            for step in (-1, 1):
                layers(step).wait()
            loop(0, 2, coefficients)
            loop(6, 8, coefficients)

        with scope("ghostcoef"):
            loop(0, 1 - (b + 3) // 4, ghost_coefficients)

        def true(i):
            step = start + i
            first = 1 - (i + 3) // 4
            final = (i + 1) // size
            edge = first + final
            deep = ((i + 3) // 4) * (1 - (i + 2) // size)
            ghost = 1 - final

            def true_h(x):
                h_pass(e, h, ah, bh, x, x + 1 + 2 * (x // 5) * (1 - x // 6), x, x)

            def true_e(x, prv):
                e_pass(e, h, j, p, q, ae, be, bm, x, x, prv, x, x)

            def more_h(x):
                store = edges_h(h, x - 1)
                true_h(x)
                store()

            store = edges_e(e, 2)
            true_h(edge)
            store()
            loop(edge + 1, 5, more_h)
            with scope("wait_e"):
                trace_e(step).wait_recv()
            take(e, 6, recv_e, step)
            loop(5, 7 - edge, more_h)

            top = 6 + ghost + deep
            store = edges_h(h, 6 - edge)
            true_e(3, 2)
            store()

            def more_e(x):
                store = edges_e(e, x - 1)
                true_e(x, x - 1)
                store()

            loop(4, top, more_e)
            with scope("wait_h"):
                trace_h(step).wait_recv()
            take(h, 1, recv_h, step)

            low = 2 - ghost - deep

            def bottom(x):
                begun = (x - low + 3) // 4
                store = edges_e(e, begun * (x - 1) + (1 - begun) * (top - 1))
                true_e(x, x - 1 + 10 * (1 - (x + 1) // 2) + 7 * (x // 2))
                store()

            loop(low, 3, bottom)

        with scope("true"):
            loop(0, size, true)
            edges_e(e, 2)()
        return carry

    lax.fori_loop(0, BLOCKS, block, 0)

    def finish(step):
        trace_e(step).wait_send()
        trace_h(step).wait_send()

    with scope("finish"):
        loop(0, STEPS, finish)

    results = [(e, c) for c in range(3)] + [(h, c) for c in range(3)]
    with scope("results"):
        for g in range(2):
            group = results[4 * g : 4 * g + 4]

            def gather(t):
                tiles = [ref[OWN + x, pl.ds(pl.multiple_of(COMP * c + TILE * (t + 1), 8), 8)] for ref, c in group for x in range(4)]
                tiles = tiles + tiles[: 16 - len(tiles)]
                whole = jnp.transpose(jnp.concatenate(tiles, 0))
                for zb in range(8):
                    turned[g, zb, pl.ds(t, 16, stride=10)] = whole[16 * zb : 16 * zb + 16]

            loop(0, TILES, gather)

            def spread(zb):
                whole = jnp.transpose(turned[g, zb, pl.ds(16, 128)])
                for s in range(len(group)):
                    for x in range(4):
                        stage[4 * g + s, zb, pl.ds(x, 8, stride=4)] = whole[32 * s + 8 * x : 32 * s + 8 * x + 8]

            loop(0, 8, spread)
            if g == 0:
                pltpu.make_async_copy(stage.at[pl.ds(0, 3)], e_out, in_sem.at[0]).start()
        pltpu.make_async_copy(stage.at[pl.ds(3, 3)], h_out, in_sem.at[1]).start()
        pltpu.make_async_copy(stage.at[pl.ds(0, 3)], e_out, in_sem.at[0]).wait()
        pltpu.make_async_copy(stage.at[pl.ds(3, 3)], h_out, in_sem.at[1]).wait()


def shards(
    e_field, h_field, drude_current, lorentz_polar, lorentz_rate, permittivity, material, absorber
):
    fields = [f.reshape(3, 8, 32, 128) for f in (e_field, h_field, drude_current, lorentz_polar, lorentz_rate)]
    cells = [c.reshape(8, 32, 128) for c in (permittivity, material, absorber)]
    wide = pltpu.VMEM((PLANES, 3 * COMP, 128), F32)
    narrow = pltpu.VMEM((PLANES, 3 * ROWS, 128), F32)
    cell = pltpu.VMEM((8, ROWS, 128), F32)
    trace = pltpu.VMEM((STEPS, 2, ROWS, 128), F32)
    out = jax.ShapeDtypeStruct((3, 8, 32, 128), F32)
    e, h = pl.pallas_call(
        kernel,
        out_shape=(out, out),
        in_specs=[pl.BlockSpec(memory_space=pl.ANY)] * 8,
        out_specs=(pl.BlockSpec(memory_space=pl.ANY),) * 2,
        scratch_shapes=[
            pltpu.VMEM((18, 8, 32, 128), F32),
            pltpu.VMEM((2, 8, 32, 128), jnp.int32),
            pltpu.VMEM((GROUPS, 8, 160, 128), F32),
            pltpu.VMEM((8, 3, ROWS, 128), F32),
            wide, wide, narrow, narrow, narrow,
            cell, cell, cell, cell, cell,
            trace, trace, trace, trace,
            pltpu.SemaphoreType.DMA((8,)),
            pltpu.SemaphoreType.DMA((2, 2 * GROUPS)),
            pltpu.SemaphoreType.DMA((2, 2)),
            pltpu.SemaphoreType.DMA((STEPS,)),
            pltpu.SemaphoreType.DMA((STEPS,)),
            pltpu.SemaphoreType.DMA((STEPS,)),
            pltpu.SemaphoreType.DMA((STEPS,)),
        ],
        compiler_params=pltpu.CompilerParams(
            collective_id=0, has_side_effects=True, vmem_limit_bytes=48 * 1024 * 1024
        ),
    )(*(pltpu.with_memory_space_constraint(a, pltpu.HBM) for a in (*fields, *cells)))
    return e.reshape(3, 64, 4, 128), h.reshape(3, 64, 4, 128)


def solution(mesh):
    field, cell = P(None, None, "gx", "gy"), P(None, "gx", "gy")
    return jax.shard_map(
        shards, mesh=mesh, in_specs=(field,) * 5 + (cell,) * 3, out_specs=(field, field), check_vma=False
    )
```

profile of v0, /device:TPU:0, one launch (start us, length us, event | category | flops | bytes accessed | tf_op | source)
XLA Modules:
  0.0 54.1 jit_solution(11189078062442026392)
XLA Ops:
  0.6 52.0 %shard_map.95 = (f32[3,8,32,128]{3,2,1,0:T(8,128)S(1)}, f32[3,8,32,128]{3,2,1,0:T(8,128)S(1)}) custom-call(f32[3,8,32,128]{3,2,1,0:T(8,128)} %bitcast.12, f32[3,8,32,128]{3,2,1,0:T(8,128)} %bitcast.13, f32[3,8,32,128]{3,2,1,0:T(8,128)} %bitcast.14, f32[3,8,32,128]{3,2,1,0:T(8,128)} %bitcast.15, f32[3,8,32,128]{3,2,1,0:T(8,128)} %bitcast.16, ...), custom_call_target="tpu_custom_call" | custom-call | tf_op jit(solution)/shard_map/pallas_call | solution.py:488
  52.7 0.7 %copy.12 = f32[3,64,4,128]{3,2,1,0:T(4,128)} copy(f32[3,64,4,128]{3,2,1,0:T(4,128)S(1)} %bitcast.11) | data formatting | bytes 786432
  53.4 0.7 %copy.13 = f32[3,64,4,128]{3,2,1,0:T(4,128)} copy(f32[3,64,4,128]{3,2,1,0:T(4,128)S(1)} %bitcast.10) | data formatting | bytes 786432
where the time goes:
time: 54.3 us; the launch traced here: 54.1 us
  Pallas kernels  52 us (96%)
  local copies, waits for them, and re-layouts  1.49 us (3%)
  between operations  0.64 us (1%)
    pallas_call x1, Pallas kernels, shards(): pl.pallas_call(kernel, out_shape=(out, out), in_specs=[pl.BlockSpec(memor...  52 us
    unnamed x2, local copies, waits for them, and re-layouts  1.49 us

commit v1 on v0

--- a/solution.py
+++ b/solution.py
@@ -29,6 +29,7 @@
 
 SLOTS = ["perm", "mat", "abs", "e0", "e1", "e2", "h0", "h1", "h2", "j0", "j1", "j2", "p0", "p1", "p2", "q0", "q1", "q2"]
 GROUPS = 5
+GHOST = STEPS
 
 
 def scope(name):
@@ -46,6 +47,10 @@
 
 def loop(low, high, body):
     lax.fori_loop(low, high, lambda i, carry: (body(i), carry)[1], 0)
+
+
+def loop_twice(count, body):
+    loop(0, count // 2, lambda i: (body(2 * i), body(2 * i + 1)))
 
 
 def at(c, t, shift=0):
@@ -64,6 +69,13 @@
         if (c, t) not in self.held:
             self.held[c, t] = self.ref[self.plane, at(c, t)]
         return self.held[c, t]
+
+
+@contextlib.contextmanager
+def later(*stores):
+    yield
+    for store in stores:
+        store()
 
 
 def pipelined(load, work):
@@ -163,6 +175,13 @@
     stage, ints, turned, raw, e, h, j, p, q, ah, bh, ae, be, bm,
     send_e, send_h, recv_e, recv_h, in_sem, y_sem, x_sem, se_sem, re_sem, sh_sem, rh_sem,
 ):
+    def blank(zb):
+        for g in range(GROUPS):
+            for edge in (0, 152):
+                turned[g, zb, pl.ds(edge, 8)] = jnp.zeros((8, 128), F32)
+
+    loop(0, 8, blank)
+
     barrier = pltpu.get_barrier_semaphore()
     for axis in ("gx", "gy"):
         for step in (-1, 1):
@@ -194,25 +213,28 @@
     clear((ZERO_H,), (h,))
 
     def turn(g):
+        slots = range(4 * g, min(4 * g + 4, len(SLOTS)))
+
         def body(zb):
             rows = []
-            for s in range(4):
-                slot = 4 * g + s
-                for x in range(4):
-                    here = pl.ds(x, 8, stride=4)
-                    if slot in (1, 2):
-                        rows.append(ints[slot - 1, zb, here].astype(F32))
-                    else:
-                        rows.append(stage[min(slot, 17), zb, here])
+            for block in (zb,) if g < 4 else (zb, zb + 4):
+                for slot in slots:
+                    for x in range(4):
+                        here = pl.ds(x, 8, stride=4)
+                        if slot in (1, 2):
+                            rows.append(ints[slot - 1, block, here].astype(F32))
+                        else:
+                            rows.append(stage[slot, block, here])
             turned[g, zb, pl.ds(16, 128)] = jnp.transpose(jnp.concatenate(rows, 0))
 
-        loop(0, 8, body)
+        loop_twice(8 if g < 4 else 4, body)
 
     def columns(g, step):
-        source, target = (pl.ds(16, 16), pl.ds(144, 16)) if step < 0 else (pl.ds(128, 16), pl.ds(0, 16))
+        source, target = (pl.ds(16, GHOST), pl.ds(144, GHOST)) if step < 0 else (pl.ds(144 - GHOST, GHOST), pl.ds(16 - GHOST, GHOST))
         k = 2 * g + (step + 1) // 2
+        blocks = pl.ds(0, 8 if g < 4 else 4)
         return pltpu.make_async_remote_copy(
-            src_ref=turned.at[g, :, source], dst_ref=turned.at[g, :, target],
+            src_ref=turned.at[g, blocks, source], dst_ref=turned.at[g, blocks, target],
             send_sem=y_sem.at[0, k], recv_sem=y_sem.at[1, k],
             device_id=towards("gy", step), device_id_type=MESH,
         )
@@ -236,8 +258,10 @@
 
     def build(g):
         def body(t):
-            rows = [turned[g, zb, pl.ds(t, 16, stride=10)] for zb in range(8)]
-            whole = jnp.transpose(jnp.concatenate(rows, 0))
+            rows = jnp.concatenate([turned[g, zb, pl.ds(t, 16, stride=10)] for zb in range(8 if g < 4 else 4)], 0)
+            if g == 4:
+                rows = jnp.concatenate([rows, pltpu.roll(rows, 64, 1)], 0)
+            whole = jnp.transpose(rows)
             for s, name in enumerate(SLOTS[4 * g : 4 * g + 4]):
                 for x in range(4):
                     part = whole[32 * s + 8 * x : 32 * s + 8 * x + 8]
@@ -253,7 +277,7 @@
                         part = part * 2.0
                     state[name[0]][OWN + x, pl.ds(pl.multiple_of(row, 8), 8)] = part
 
-        loop(0, TILES, body)
+        loop_twice(TILES, body)
 
     def layers(step):
         source, target = (OWN, OWN + 4) if step < 0 else (OWN + 2, OWN - 2)
@@ -321,55 +345,54 @@
         size = 4 - b // 2
         start = 4 * b - b // 3
 
-        def free_h(x, base):
-            nxt = base + x + 1 + (x // 3) * (ZERO_E - base - 4)
-            h_pass(e, h, ah, bh, base + x, nxt, FREE + x, OWN + x)
-
-        def free_e(x, base):
-            e_pass(e, h, j, p, q, ae, be, bm, base + x, FREE + x, FREE + x - 1, FREE + x, OWN + x)
+        def free_h(x, src, dst):
+            nxt = src + x + 1 + (x // 3) * (ZERO_E - src - 4)
+            h_pass(e, h, ah, bh, src + x, nxt, dst + x, OWN + x)
+
+        def free_e(x, src, dst):
+            prv = dst + x - 1 + (1 - (x + 2) // 3) * (ZERO_H - dst + 1)
+            e_pass(e, h, j, p, q, ae, be, bm, src + x, dst + x, prv, dst + x, OWN + x)
 
         def give_e(plane, step):
             give(e, plane, send_e, step)
             trace_e(step).start()
 
-        def give_h(step):
-            give(h, FREE + 3, send_h, step)
+        def give_h(plane, step):
+            give(h, plane, send_h, step)
             trace_h(step).start()
 
         def free(i):
-            base = OWN + ((i + 3) // 4) * (FREE - OWN)
+            src = OWN + (i // 2) * (FREE - OWN)
+            dst = OWN + ((i + 3) // 4) * (FREE - OWN)
             last = (i + 2) // size
-            give_e(base, start + i)
-            store = edges_e(e, base + 2)
-            free_h(3, base)
-            store()
-            give_h(start + i)
-
-            def more_h(x):
-                store = edges_h(h, FREE + x - 1 + 4 * (1 - (x + 2) // 3))
-                free_h(x, base)
-                store()
-
-            loop(0, 3, more_h)
-            store = edges_h(h, FREE + 2)
-            free_e(3, base)
-            store()
-
-            def more_e(x):
-                store = edges_e(e, FREE + x - 1 + 4 * (1 - (x + 2) // 3))
-                free_e(x, base)
-                store()
-
-            loop(0, 3 - 2 * last, more_e)
+            give_e(src, start + i)
+            with later(*(edges_e(e, src + x) for x in range(3))):
+                free_h(3, src, dst)
+            give_h(dst + 3, start + i)
+            with later(edges_h(h, dst + 3)):
+                free_h(0, src, dst)
+                free_h(1, src, dst)
+                free_h(2, src, dst)
+            with later(edges_h(h, dst)):
+                free_e(3, src, dst)
+            with later(edges_e(e, dst + 3), edges_h(h, dst + 1), edges_h(h, dst + 2)):
+                free_e(0, src, dst)
+
+            def inner(_):
+                free_e(1, src, dst)
+                free_e(2, src, dst)
+
+            loop(last, 1, inner)
 
         with scope("free"):
             loop(0, size - 1, free)
             give_e(FREE, start + size - 1)
-            free_h(3, FREE)
-            give_h(start + size - 1)
+            free_h(3, FREE, FREE)
+            give_h(FREE + 3, start + size - 1)
 
         with scope("clear"):
-            clear((0, 1, 6, 7), (e, h, j, p, q))
+            clear((0, 1, 6, 7), (e, h))
+            clear((1, 6), (j, p, q))
 
         def ghost_coefficients(i):
             for step in (-1, 1):
@@ -380,62 +403,89 @@
         with scope("ghostcoef"):
             loop(0, 1 - (b + 3) // 4, ghost_coefficients)
 
+        def from_own(cell, mag, plane):
+            for t in range(TILES):
+                b = be[cell, pl.ds(8 * t, 8)]
+                hy, hz = h[mag, at(1, t)], h[mag, at(2, t)]
+                curl = (hz - h[mag, at(2, t - 1)]) - (hy - h[mag, at(1, t, -1)])
+                e[plane, at(0, t)] = e[plane, at(0, t)] + b * curl
+                e[plane, at(1, t)] = e[plane, at(1, t)] - b * hz
+                e[plane, at(2, t)] = e[plane, at(2, t)] + b * hy
+
+        def from_below(mag, plane):
+            for t in range(TILES):
+                b = be[plane, pl.ds(8 * t, 8)]
+                e[plane, at(1, t)] = b * h[mag, at(2, t)]
+                e[plane, at(2, t)] = -b * h[mag, at(1, t)]
+
+        def answer(trace, cell, delta, plane):
+            for t in range(TILES):
+                here = pl.ds(8 * t, 8)
+                b = bh[cell, here]
+                hy, hz = b * trace[start, 1, here], b * trace[start, 0, here]
+                h[delta, at(1, t)] = hy
+                h[delta, at(2, t)] = -hz
+                if delta != plane:
+                    h[plane, at(1, t)] = h[plane, at(1, t)] + hy
+                    h[plane, at(2, t)] = h[plane, at(2, t)] - hz
+            edges_h(h, delta)()
+            from_own(cell, delta, plane)
+
+        with scope("first"):
+            answer(send_e, 1, 1, 1)
+            with scope("wait_e"):
+                trace_e(start).wait_recv()
+            answer(recv_e, 5, FREE + 3, 5)
+            from_below(5, 6)
+            with scope("wait_h"):
+                trace_h(start).wait_recv()
+            for t in range(TILES):
+                here = pl.ds(8 * t, 8)
+                b = be[2, here]
+                e[2, at(1, t)] = e[2, at(1, t)] + b * (h[1, at(2, t)] + recv_h[start, 1, here])
+                e[2, at(2, t)] = e[2, at(2, t)] - b * (h[1, at(1, t)] + recv_h[start, 0, here])
+
         def true(i):
             step = start + i
-            first = 1 - (i + 3) // 4
             final = (i + 1) // size
-            edge = first + final
-            deep = ((i + 3) // 4) * (1 - (i + 2) // size)
-            ghost = 1 - final
-
-            def true_h(x):
-                h_pass(e, h, ah, bh, x, x + 1 + 2 * (x // 5) * (1 - x // 6), x, x)
+            deep = 1 - (i + 2) // size
+
+            def true_h(x, nxt):
+                h_pass(e, h, ah, bh, x, nxt, x, x)
 
             def true_e(x, prv):
                 e_pass(e, h, j, p, q, ae, be, bm, x, x, prv, x, x)
 
-            def more_h(x):
-                store = edges_h(h, x - 1)
-                true_h(x)
-                store()
-
-            store = edges_e(e, 2)
-            true_h(edge)
-            store()
-            loop(edge + 1, 5, more_h)
+            with later(*(edges_e(e, x) for x in (0, 1, 2, 5, 6))):
+                true_h(3, 4)
+                true_h(4, 5)
+            with later(edges_h(h, 3), edges_h(h, 4)):
+                true_h(1, 2)
+                true_h(2, 3)
+            loop(final, 1, lambda _: true_h(0, 1))
             with scope("wait_e"):
                 trace_e(step).wait_recv()
             take(e, 6, recv_e, step)
-            loop(5, 7 - edge, more_h)
-
-            top = 6 + ghost + deep
-            store = edges_h(h, 6 - edge)
-            true_e(3, 2)
-            store()
-
-            def more_e(x):
-                store = edges_e(e, x - 1)
-                true_e(x, x - 1)
-                store()
-
-            loop(4, top, more_e)
+            true_h(5, CROSS)
+            loop(final, 1, lambda _: true_h(6, 7))
+
+            with later(*(edges_h(h, x) for x in (1, 2, 5, 6))):
+                true_e(3, 2)
+                true_e(4, 3)
+            with later(edges_e(e, 3), edges_e(e, 4), edges_h(h, 0)):
+                true_e(5, 4)
+            loop(final, 1, lambda _: true_e(6, 5))
+            loop(1 - deep, 1, lambda _: from_below(6, 7))
             with scope("wait_h"):
                 trace_h(step).wait_recv()
             take(h, 1, recv_h, step)
-
-            low = 2 - ghost - deep
-
-            def bottom(x):
-                begun = (x - low + 3) // 4
-                store = edges_e(e, begun * (x - 1) + (1 - begun) * (top - 1))
-                true_e(x, x - 1 + 10 * (1 - (x + 1) // 2) + 7 * (x // 2))
-                store()
-
-            loop(low, 3, bottom)
+            with later(edges_e(e, 5)):
+                true_e(2, CROSS)
+            loop(final, 1, lambda _: true_e(1, 0))
+            loop(1 - deep, 1, lambda _: from_own(0, 0, 0))
 
         with scope("true"):
-            loop(0, size, true)
-            edges_e(e, 2)()
+            loop(1, size, true)
         return carry
 
     lax.fori_loop(0, BLOCKS, block, 0)
@@ -459,7 +509,7 @@
                 for zb in range(8):
                     turned[g, zb, pl.ds(t, 16, stride=10)] = whole[16 * zb : 16 * zb + 16]
 
-            loop(0, TILES, gather)
+            loop_twice(TILES, gather)
 
             def spread(zb):
                 whole = jnp.transpose(turned[g, zb, pl.ds(16, 128)])
@@ -467,7 +517,7 @@
                     for x in range(4):
                         stage[4 * g + s, zb, pl.ds(x, 8, stride=4)] = whole[32 * s + 8 * x : 32 * s + 8 * x + 8]
 
-            loop(0, 8, spread)
+            loop_twice(8, spread)
             if g == 0:
                 pltpu.make_async_copy(stage.at[pl.ds(0, 3)], e_out, in_sem.at[0]).start()
         pltpu.make_async_copy(stage.at[pl.ds(3, 3)], h_out, in_sem.at[1]).start()

time: 54.3 us -> 47 us (0.87)
  Pallas kernels: 52 us -> 44.7 us
    pallas_call x1, Pallas kernels: 52 us -> 44.7 us  [shards(): pl.pallas_call(kernel, out_shape=(out, out), in_specs=[pl.BlockSpec(memor...]
where the time goes in v1:
time: 47 us; the launch traced here: 46.8 us
  Pallas kernels  44.7 us (95%)
  local copies, waits for them, and re-layouts  1.49 us (3%)
  between operations  0.64 us (1%)
    pallas_call x1, Pallas kernels, shards(): pl.pallas_call(kernel, out_shape=(out, out), in_specs=[pl.BlockSpec(memor...  44.7 us
    unnamed x2, local copies, waits for them, and re-layouts  1.49 us

profile of v1, /device:TPU:0, one launch (start us, length us, event | category | flops | bytes accessed | tf_op | source)
XLA Modules:
  0.0 46.8 jit_solution(10268895853767512716)
XLA Ops:
  0.6 44.7 %shard_map.95 = (f32[3,8,32,128]{3,2,1,0:T(8,128)S(1)}, f32[3,8,32,128]{3,2,1,0:T(8,128)S(1)}) custom-call(f32[3,8,32,128]{3,2,1,0:T(8,128)} %bitcast.12, f32[3,8,32,128]{3,2,1,0:T(8,128)} %bitcast.13, f32[3,8,32,128]{3,2,1,0:T(8,128)} %bitcast.14, f32[3,8,32,128]{3,2,1,0:T(8,128)} %bitcast.15, f32[3,8,32,128]{3,2,1,0:T(8,128)} %bitcast.16, ...), custom_call_target="tpu_custom_call" | custom-call | tf_op jit(solution)/shard_map/pallas_call | solution.py:538
  45.3 0.7 %copy.12 = f32[3,64,4,128]{3,2,1,0:T(4,128)} copy(f32[3,64,4,128]{3,2,1,0:T(4,128)S(1)} %bitcast.11) | data formatting | bytes 786432
  46.1 0.7 %copy.13 = f32[3,64,4,128]{3,2,1,0:T(4,128)} copy(f32[3,64,4,128]{3,2,1,0:T(4,128)S(1)} %bitcast.10) | data formatting | bytes 786432

commit v2 on v1

--- a/solution.py
+++ b/solution.py
@@ -173,7 +173,7 @@
 def kernel(
     e_in, h_in, j_in, p_in, q_in, perm_in, mat_in, abs_in, e_out, h_out,
     stage, ints, turned, raw, e, h, j, p, q, ah, bh, ae, be, bm,
-    send_e, send_h, recv_e, recv_h, in_sem, y_sem, x_sem, se_sem, re_sem, sh_sem, rh_sem,
+    send_e, send_h, recv_e, recv_h, in_sem, y_sem, x_sem, s_sem, re_sem, rh_sem,
 ):
     def blank(zb):
         for g in range(GROUPS):
@@ -188,15 +188,14 @@
             pl.semaphore_signal(barrier, inc=1, device_id=towards(axis, step), device_id_type=MESH)
 
     fields = (e_in, h_in, j_in, p_in, q_in)
-    loads = {
-        "perm": pltpu.make_async_copy(perm_in, stage.at[0], in_sem.at[5]),
-        "mat": pltpu.make_async_copy(mat_in, ints.at[0], in_sem.at[6]),
-        "abs": pltpu.make_async_copy(abs_in, ints.at[1], in_sem.at[7]),
-    }
+    pltpu.make_async_copy(perm_in, stage.at[0], in_sem.at[0]).start()
+    pltpu.make_async_copy(mat_in, ints.at[0], in_sem.at[0]).start()
+    pltpu.make_async_copy(abs_in, ints.at[1], in_sem.at[0]).start()
     for i, f in enumerate(fields):
-        loads["ehjpq"[i]] = pltpu.make_async_copy(f, stage.at[pl.ds(3 + 3 * i, 3)], in_sem.at[i])
-    for load in loads.values():
-        load.start()
+        pltpu.make_async_copy(f, stage.at[pl.ds(3 + 3 * i, 3)], in_sem.at[i]).start()
+
+    def arrive(ref, sem):
+        pltpu.make_async_copy(ref, ref, sem).wait()
 
     def clear(planes, refs):
         for ref in refs:
@@ -231,22 +230,19 @@
 
     def columns(g, step):
         source, target = (pl.ds(16, GHOST), pl.ds(144, GHOST)) if step < 0 else (pl.ds(144 - GHOST, GHOST), pl.ds(16 - GHOST, GHOST))
-        k = 2 * g + (step + 1) // 2
         blocks = pl.ds(0, 8 if g < 4 else 4)
         return pltpu.make_async_remote_copy(
             src_ref=turned.at[g, blocks, source], dst_ref=turned.at[g, blocks, target],
-            send_sem=y_sem.at[0, k], recv_sem=y_sem.at[1, k],
+            send_sem=y_sem.at[GROUPS], recv_sem=y_sem.at[g],
             device_id=towards("gy", step), device_id_type=MESH,
         )
 
-    waited = set()
     for g in range(GROUPS):
         with scope("turn"):
-            for name in SLOTS[4 * g : 4 * g + 4]:
-                name = name if name in loads else name[0]
-                if name not in waited:
-                    waited.add(name)
-                    loads[name].wait()
+            if g < 4:
+                arrive(stage.at[pl.ds(0, 6)] if g == 0 else stage.at[pl.ds(3 + 3 * g, 3)], in_sem.at[g])
+            if g == 3:
+                arrive(stage.at[pl.ds(15, 3)], in_sem.at[4])
             turn(g)
         if g == 0:
             with scope("barrier"):
@@ -281,10 +277,9 @@
 
     def layers(step):
         source, target = (OWN, OWN + 4) if step < 0 else (OWN + 2, OWN - 2)
-        k = (step + 1) // 2
         return pltpu.make_async_remote_copy(
             src_ref=raw.at[pl.ds(source, 2)], dst_ref=raw.at[pl.ds(target, 2)],
-            send_sem=x_sem.at[0, k], recv_sem=x_sem.at[1, k],
+            send_sem=x_sem.at[0], recv_sem=x_sem.at[1],
             device_id=towards("gx", step), device_id_type=MESH,
         )
 
@@ -304,10 +299,59 @@
             be[plane, here] = b
             bm[plane, here] = jnp.where(mat == 2.0, 0.5 * b, 0.0)
 
+    def trace_e(step, mark):
+        return pltpu.make_async_remote_copy(
+            src_ref=send_e.at[step], dst_ref=recv_e.at[step],
+            send_sem=s_sem.at[0], recv_sem=re_sem.at[mark],
+            device_id=towards("gx", -1), device_id_type=MESH,
+        )
+
+    def trace_h(step, mark):
+        return pltpu.make_async_remote_copy(
+            src_ref=send_h.at[step], dst_ref=recv_h.at[step],
+            send_sem=s_sem.at[1], recv_sem=rh_sem.at[mark],
+            device_id=towards("gx", 1), device_id_type=MESH,
+        )
+
+    def give(ref, plane, out, step):
+        for c in range(2):
+            for t in range(TILES):
+                out[step, c, pl.ds(8 * t, 8)] = ref[plane, at(1 + c, t)]
+
+    def take(ref, plane, trace, step):
+        for c in range(2):
+            for t in range(TILES):
+                ref[CROSS, at(1 + c, t)] = ref[plane, at(1 + c, t)] + trace[step, c, pl.ds(8 * t, 8)]
+
+    def free_h(x, src, dst):
+        nxt = src + x + 1 + (x // 3) * (ZERO_E - src - 4)
+        h_pass(e, h, ah, bh, src + x, nxt, dst + x, OWN + x)
+
+    def free_e(x, src, dst):
+        prv = dst + x - 1 + (1 - (x + 2) // 3) * (ZERO_H - dst + 1)
+        e_pass(e, h, j, p, q, ae, be, bm, src + x, dst + x, prv, dst + x, OWN + x)
+
+    def give_e(plane, step, mark):
+        give(e, plane, send_e, step)
+        trace_e(step, mark).start()
+
+    def give_h(plane, step, mark):
+        give(h, plane, send_h, step)
+        trace_h(step, mark).start()
+
+    def h_part(src, dst, step, mark):
+        give_e(src, step, mark)
+        with later(*(edges_e(e, src + x) for x in range(3))):
+            free_h(3, src, dst)
+        give_h(dst + 3, step, mark)
+        with later(edges_h(h, dst + 3)):
+            free_h(0, src, dst)
+            free_h(1, src, dst)
+            free_h(2, src, dst)
+
     for g in range(GROUPS):
         with scope("ghosts"):
-            for step in (-1, 1):
-                columns(g, step).wait()
+            arrive(turned.at[g, pl.ds(0, 8 if g < 4 else 4), pl.ds(0, 2 * GHOST)], y_sem.at[g])
         with scope("build"):
             build(g)
         if g == 0:
@@ -316,63 +360,19 @@
             loop(OWN, OWN + 4, coefficients)
         if g == 1:
             loop(OWN, OWN + 4, lambda x: edges_e(e, x)())
-
-    def trace_e(step):
-        return pltpu.make_async_remote_copy(
-            src_ref=send_e.at[step], dst_ref=recv_e.at[step],
-            send_sem=se_sem.at[step], recv_sem=re_sem.at[step],
-            device_id=towards("gx", -1), device_id_type=MESH,
-        )
-
-    def trace_h(step):
-        return pltpu.make_async_remote_copy(
-            src_ref=send_h.at[step], dst_ref=recv_h.at[step],
-            send_sem=sh_sem.at[step], recv_sem=rh_sem.at[step],
-            device_id=towards("gx", 1), device_id_type=MESH,
-        )
-
-    def give(ref, plane, out, step):
-        for c in range(2):
-            for t in range(TILES):
-                out[step, c, pl.ds(8 * t, 8)] = ref[plane, at(1 + c, t)]
-
-    def take(ref, plane, trace, step):
-        for c in range(2):
-            for t in range(TILES):
-                ref[CROSS, at(1 + c, t)] = ref[plane, at(1 + c, t)] + trace[step, c, pl.ds(8 * t, 8)]
+        if g == 2:
+            h_part(OWN, OWN, 0, 0)
 
     def block(b, carry):
         size = 4 - b // 2
         start = 4 * b - b // 3
-
-        def free_h(x, src, dst):
-            nxt = src + x + 1 + (x // 3) * (ZERO_E - src - 4)
-            h_pass(e, h, ah, bh, src + x, nxt, dst + x, OWN + x)
-
-        def free_e(x, src, dst):
-            prv = dst + x - 1 + (1 - (x + 2) // 3) * (ZERO_H - dst + 1)
-            e_pass(e, h, j, p, q, ae, be, bm, src + x, dst + x, prv, dst + x, OWN + x)
-
-        def give_e(plane, step):
-            give(e, plane, send_e, step)
-            trace_e(step).start()
-
-        def give_h(plane, step):
-            give(h, plane, send_h, step)
-            trace_h(step).start()
+        marks = 4 * lax.rem(b, 2) - start
 
         def free(i):
             src = OWN + (i // 2) * (FREE - OWN)
             dst = OWN + ((i + 3) // 4) * (FREE - OWN)
             last = (i + 2) // size
-            give_e(src, start + i)
-            with later(*(edges_e(e, src + x) for x in range(3))):
-                free_h(3, src, dst)
-            give_h(dst + 3, start + i)
-            with later(edges_h(h, dst + 3)):
-                free_h(0, src, dst)
-                free_h(1, src, dst)
-                free_h(2, src, dst)
+            loop(1 - (i + 3) // 4, 1, lambda _: h_part(src, dst, start + i, marks + start + i))
             with later(edges_h(h, dst)):
                 free_e(3, src, dst)
             with later(edges_e(e, dst + 3), edges_h(h, dst + 1), edges_h(h, dst + 2)):
@@ -386,17 +386,17 @@
 
         with scope("free"):
             loop(0, size - 1, free)
-            give_e(FREE, start + size - 1)
+            final = start + size - 1
+            give_e(FREE, final, marks + final)
             free_h(3, FREE, FREE)
-            give_h(FREE + 3, start + size - 1)
+            give_h(FREE + 3, final, marks + final)
 
         with scope("clear"):
             clear((0, 1, 6, 7), (e, h))
             clear((1, 6), (j, p, q))
 
         def ghost_coefficients(i):
-            for step in (-1, 1):
-                layers(step).wait()
+            arrive(raw.at[pl.ds(0, 4)], x_sem.at[1])
             loop(0, 2, coefficients)
             loop(6, 8, coefficients)
 
@@ -434,16 +434,16 @@
         with scope("first"):
             answer(send_e, 1, 1, 1)
             with scope("wait_e"):
-                trace_e(start).wait_recv()
+                trace_e(start, marks + start).wait_recv()
             answer(recv_e, 5, FREE + 3, 5)
             from_below(5, 6)
             with scope("wait_h"):
-                trace_h(start).wait_recv()
+                trace_h(start, marks + start).wait_recv()
             for t in range(TILES):
                 here = pl.ds(8 * t, 8)
-                b = be[2, here]
-                e[2, at(1, t)] = e[2, at(1, t)] + b * (h[1, at(2, t)] + recv_h[start, 1, here])
-                e[2, at(2, t)] = e[2, at(2, t)] - b * (h[1, at(1, t)] + recv_h[start, 0, here])
+                own = be[2, here]
+                e[2, at(1, t)] = e[2, at(1, t)] + own * (h[1, at(2, t)] + recv_h[start, 1, here])
+                e[2, at(2, t)] = e[2, at(2, t)] - own * (h[1, at(1, t)] + recv_h[start, 0, here])
 
         def true(i):
             step = start + i
@@ -464,7 +464,7 @@
                 true_h(2, 3)
             loop(final, 1, lambda _: true_h(0, 1))
             with scope("wait_e"):
-                trace_e(step).wait_recv()
+                trace_e(step, marks + step).wait_recv()
             take(e, 6, recv_e, step)
             true_h(5, CROSS)
             loop(final, 1, lambda _: true_h(6, 7))
@@ -477,7 +477,7 @@
             loop(final, 1, lambda _: true_e(6, 5))
             loop(1 - deep, 1, lambda _: from_below(6, 7))
             with scope("wait_h"):
-                trace_h(step).wait_recv()
+                trace_h(step, marks + step).wait_recv()
             take(h, 1, recv_h, step)
             with later(edges_e(e, 5)):
                 true_e(2, CROSS)
@@ -486,18 +486,23 @@
 
         with scope("true"):
             loop(1, size, true)
+
+        def onward(_):
+            h_part(OWN, OWN, start + size, 4 * lax.rem(b + 1, 2))
+
+        loop(b // 3, 1, onward)
         return carry
 
     lax.fori_loop(0, BLOCKS, block, 0)
 
-    def finish(step):
-        trace_e(step).wait_send()
-        trace_h(step).wait_send()
-
     with scope("finish"):
-        loop(0, STEPS, finish)
+        arrive(send_e, s_sem.at[0])
+        arrive(send_h, s_sem.at[1])
+        arrive(raw.at[pl.ds(0, 4)], x_sem.at[0])
+        arrive(turned.at[0, :, pl.ds(0, 9 * GHOST)], y_sem.at[GROUPS])
 
     results = [(e, c) for c in range(3)] + [(h, c) for c in range(3)]
+    outs = [(e_out, c) for c in range(3)] + [(h_out, c) for c in range(3)]
     with scope("results"):
         for g in range(2):
             group = results[4 * g : 4 * g + 4]
@@ -515,14 +520,21 @@
                 whole = jnp.transpose(turned[g, zb, pl.ds(16, 128)])
                 for s in range(len(group)):
                     for x in range(4):
-                        stage[4 * g + s, zb, pl.ds(x, 8, stride=4)] = whole[32 * s + 8 * x : 32 * s + 8 * x + 8]
+                        out, c = outs[4 * g + s]
+                        out[c, zb, pl.ds(x, 8, stride=4)] = whole[32 * s + 8 * x : 32 * s + 8 * x + 8]
 
             loop_twice(8, spread)
-            if g == 0:
-                pltpu.make_async_copy(stage.at[pl.ds(0, 3)], e_out, in_sem.at[0]).start()
-        pltpu.make_async_copy(stage.at[pl.ds(3, 3)], h_out, in_sem.at[1]).start()
-        pltpu.make_async_copy(stage.at[pl.ds(0, 3)], e_out, in_sem.at[0]).wait()
-        pltpu.make_async_copy(stage.at[pl.ds(3, 3)], h_out, in_sem.at[1]).wait()
+
+def hand_out(e, h, e_out, h_out, sem):
+    copies = [
+        pltpu.make_async_copy(ref.at[c], out.at[c], sem.at[3 * i + c])
+        for i, (ref, out) in enumerate(((e, e_out), (h, h_out)))
+        for c in range(3)
+    ]
+    for copy in copies:
+        copy.start()
+    for copy in copies:
+        copy.wait()
 
 
 def shards(
@@ -534,12 +546,11 @@
     narrow = pltpu.VMEM((PLANES, 3 * ROWS, 128), F32)
     cell = pltpu.VMEM((8, ROWS, 128), F32)
     trace = pltpu.VMEM((STEPS, 2, ROWS, 128), F32)
-    out = jax.ShapeDtypeStruct((3, 8, 32, 128), F32)
     e, h = pl.pallas_call(
         kernel,
-        out_shape=(out, out),
+        out_shape=(pltpu.VMEM((3, 8, 32, 128), F32),) * 2,
         in_specs=[pl.BlockSpec(memory_space=pl.ANY)] * 8,
-        out_specs=(pl.BlockSpec(memory_space=pl.ANY),) * 2,
+        out_specs=(pl.BlockSpec(memory_space=pltpu.VMEM),) * 2,
         scratch_shapes=[
             pltpu.VMEM((18, 8, 32, 128), F32),
             pltpu.VMEM((2, 8, 32, 128), jnp.int32),
@@ -548,18 +559,24 @@
             wide, wide, narrow, narrow, narrow,
             cell, cell, cell, cell, cell,
             trace, trace, trace, trace,
+            pltpu.SemaphoreType.DMA((5,)),
+            pltpu.SemaphoreType.DMA((GROUPS + 1,)),
+            pltpu.SemaphoreType.DMA((2,)),
+            pltpu.SemaphoreType.DMA((2,)),
             pltpu.SemaphoreType.DMA((8,)),
-            pltpu.SemaphoreType.DMA((2, 2 * GROUPS)),
-            pltpu.SemaphoreType.DMA((2, 2)),
-            pltpu.SemaphoreType.DMA((STEPS,)),
-            pltpu.SemaphoreType.DMA((STEPS,)),
-            pltpu.SemaphoreType.DMA((STEPS,)),
-            pltpu.SemaphoreType.DMA((STEPS,)),
+            pltpu.SemaphoreType.DMA((8,)),
         ],
         compiler_params=pltpu.CompilerParams(
             collective_id=0, has_side_effects=True, vmem_limit_bytes=48 * 1024 * 1024
         ),
     )(*(pltpu.with_memory_space_constraint(a, pltpu.HBM) for a in (*fields, *cells)))
+    e, h = pl.pallas_call(
+        hand_out,
+        out_shape=(jax.ShapeDtypeStruct((3, 8, 32, 128), F32),) * 2,
+        in_specs=[pl.BlockSpec(memory_space=pltpu.VMEM)] * 2,
+        out_specs=(pl.BlockSpec(memory_space=pltpu.HBM),) * 2,
+        scratch_shapes=[pltpu.SemaphoreType.DMA((6,))],
+    )(*(pltpu.with_memory_space_constraint(a, pltpu.VMEM) for a in (e, h)))
     return e.reshape(3, 64, 4, 128), h.reshape(3, 64, 4, 128)
 
 

time: 47 us -> 45.2 us (0.962)
  local copies, waits for them, and re-layouts: 1.49 us -> 0 us
    unnamed x2 -> x0, local copies, waits for them, and re-layouts: 1.49 us -> none
    pallas_call x1 -> x2, Pallas kernels: 44.7 us -> 44.4 us  [the longest x1 43.5 us: shards(): pl.pallas_call(kernel, out_shape=(pltpu.VMEM((3, 8, 32, 128), F32),) * 2,...]
where the time goes in v2:
time: 45.2 us; the launch traced here: 45 us
  Pallas kernels  44.4 us (98%)
  between operations  0.64 us (1%)
    pallas_call x1, Pallas kernels, shards(): pl.pallas_call(kernel, out_shape=(pltpu.VMEM((3, 8, 32, 128), F32),) * 2,...  43.5 us
    pallas_call x1, Pallas kernels, shards(): pl.pallas_call(hand_out, out_shape=(jax.ShapeDtypeStruct((3, 8, 32, 128),...  0.93 us

profile of v2, /device:TPU:0, one launch (start us, length us, event | category | flops | bytes accessed | tf_op | source)
XLA Modules:
  0.0 45.0 jit_solution(17234453579552121858)
XLA Ops:
  0.6 43.5 %shard_map.95 = (f32[3,8,32,128]{3,2,1,0:T(8,128)S(1)}, f32[3,8,32,128]{3,2,1,0:T(8,128)S(1)}) custom-call(f32[3,8,32,128]{3,2,1,0:T(8,128)} %bitcast.10, f32[3,8,32,128]{3,2,1,0:T(8,128)} %bitcast.11, f32[3,8,32,128]{3,2,1,0:T(8,128)} %bitcast.12, f32[3,8,32,128]{3,2,1,0:T(8,128)} %bitcast.13, f32[3,8,32,128]{3,2,1,0:T(8,128)} %bitcast.14, ...), custom_call_target="tpu_custom_call" | custom-call | tf_op jit(solution)/shard_map/pallas_call | solution.py:549
  44.1 0.9 %shard_map.96 = (f32[3,8,32,128]{3,2,1,0:T(8,128)}, f32[3,8,32,128]{3,2,1,0:T(8,128)}) custom-call(f32[3,8,32,128]{3,2,1,0:T(8,128)S(1)} %get-tuple-element.6.e, f32[3,8,32,128]{3,2,1,0:T(8,128)S(1)} %get-tuple-element.7.h), custom_call_target="tpu_custom_call" | custom-call | tf_op jit(solution)/shard_map/pallas_call | solution.py:573

commit v3 on v2

--- a/solution.py
+++ b/solution.py
@@ -49,8 +49,8 @@
     lax.fori_loop(low, high, lambda i, carry: (body(i), carry)[1], 0)
 
 
-def loop_twice(count, body):
-    loop(0, count // 2, lambda i: (body(2 * i), body(2 * i + 1)))
+def loop_by(size, count, body):
+    loop(0, count // size, lambda i: [body(size * i + k) for k in range(size)])
 
 
 def at(c, t, shift=0):
@@ -226,7 +226,7 @@
                             rows.append(stage[slot, block, here])
             turned[g, zb, pl.ds(16, 128)] = jnp.transpose(jnp.concatenate(rows, 0))
 
-        loop_twice(8 if g < 4 else 4, body)
+        loop_by(2, 8 if g < 4 else 4, body)
 
     def columns(g, step):
         source, target = (pl.ds(16, GHOST), pl.ds(144, GHOST)) if step < 0 else (pl.ds(144 - GHOST, GHOST), pl.ds(16 - GHOST, GHOST))
@@ -257,6 +257,7 @@
             rows = jnp.concatenate([turned[g, zb, pl.ds(t, 16, stride=10)] for zb in range(8 if g < 4 else 4)], 0)
             if g == 4:
                 rows = jnp.concatenate([rows, pltpu.roll(rows, 64, 1)], 0)
+                rows = rows[:, :64]
             whole = jnp.transpose(rows)
             for s, name in enumerate(SLOTS[4 * g : 4 * g + 4]):
                 for x in range(4):
@@ -273,25 +274,25 @@
                         part = part * 2.0
                     state[name[0]][OWN + x, pl.ds(pl.multiple_of(row, 8), 8)] = part
 
-        loop_twice(TILES, body)
-
-    def layers(step):
-        source, target = (OWN, OWN + 4) if step < 0 else (OWN + 2, OWN - 2)
+        loop_by(2 if g < 4 else 5, TILES, body)
+
+    def layer(source, target, step, k):
         return pltpu.make_async_remote_copy(
-            src_ref=raw.at[pl.ds(source, 2)], dst_ref=raw.at[pl.ds(target, 2)],
-            send_sem=x_sem.at[0], recv_sem=x_sem.at[1],
+            src_ref=source, dst_ref=target, send_sem=x_sem.at[3], recv_sem=x_sem.at[k],
             device_id=towards("gx", step), device_id_type=MESH,
         )
 
-    def coefficients(plane):
+    def coefficients(plane, h_alone=False):
         for t in range(TILES):
             here = pl.ds(8 * t, 8)
-            perm, mat, absorb = (raw[plane, i, here] for i in range(3))
-            s = 0.1 * absorb
-            eff = jnp.where(mat == 0.0, 1.0, perm)
+            s = 0.1 * raw[plane, 2, here]
             r = 1.0 / (1.0 + s)
             ah[plane, here] = (1.0 - s) * r
             bh[plane, here] = 0.5 * r
+            if h_alone:
+                continue
+            perm, mat = raw[plane, 0, here], raw[plane, 1, here]
+            eff = jnp.where(mat == 0.0, 1.0, perm)
             se = s / eff
             r = 1.0 / (1.0 + se)
             ae[plane, here] = (1.0 - se) * r
@@ -355,17 +356,20 @@
         with scope("build"):
             build(g)
         if g == 0:
-            for step in (-1, 1):
-                layers(step).start()
+            layer(raw.at[OWN], raw.at[OWN + 4], -1, 0).start()
+            layer(raw.at[OWN + 3], raw.at[OWN - 1], 1, 0).start()
+            layer(raw.at[OWN + 2, 2], raw.at[OWN - 2, 2], 1, 1).start()
             loop(OWN, OWN + 4, coefficients)
         if g == 1:
             loop(OWN, OWN + 4, lambda x: edges_e(e, x)())
         if g == 2:
             h_part(OWN, OWN, 0, 0)
+            layer(be.at[OWN + 1], be.at[OWN + 5], -1, 2).start()
+            layer(be.at[OWN + 2], be.at[OWN - 2], 1, 2).start()
 
     def block(b, carry):
-        size = 4 - b // 2
-        start = 4 * b - b // 3
+        size = 3 + b // 2
+        start = 3 * b + b // 3
         marks = 4 * lax.rem(b, 2) - start
 
         def free(i):
@@ -395,13 +399,16 @@
             clear((0, 1, 6, 7), (e, h))
             clear((1, 6), (j, p, q))
 
-        def ghost_coefficients(i):
-            arrive(raw.at[pl.ds(0, 4)], x_sem.at[1])
-            loop(0, 2, coefficients)
-            loop(6, 8, coefficients)
+        def ghost_coefficients(_):
+            arrive(raw.at[pl.ds(0, 2)], x_sem.at[0])
+            coefficients(1)
+            coefficients(6)
+            arrive(raw.at[0, 2], x_sem.at[1])
+            coefficients(0, h_alone=True)
 
         with scope("ghostcoef"):
-            loop(0, 1 - (b + 3) // 4, ghost_coefficients)
+            loop((b + 3) // 4, 1, ghost_coefficients)
+            loop(1 - (b // 2) * (1 - b // 3), 1, lambda _: arrive(be.at[pl.ds(0, 2)], x_sem.at[2]))
 
         def from_own(cell, mag, plane):
             for t in range(TILES):
@@ -463,17 +470,19 @@
                 true_h(1, 2)
                 true_h(2, 3)
             loop(final, 1, lambda _: true_h(0, 1))
+            with later(edges_h(h, 0), edges_h(h, 1), edges_h(h, 2)):
+                true_e(3, 2)
+                true_e(4, 3)
+            loop(final, 1, lambda _: true_e(1, 0))
             with scope("wait_e"):
                 trace_e(step, marks + step).wait_recv()
             take(e, 6, recv_e, step)
-            true_h(5, CROSS)
+            with later(edges_e(e, 3), edges_e(e, 4)):
+                true_h(5, CROSS)
             loop(final, 1, lambda _: true_h(6, 7))
-
-            with later(*(edges_h(h, x) for x in (1, 2, 5, 6))):
-                true_e(3, 2)
-                true_e(4, 3)
-            with later(edges_e(e, 3), edges_e(e, 4), edges_h(h, 0)):
-                true_e(5, 4)
+            for store in (edges_h(h, 5), edges_h(h, 6)):
+                store()
+            true_e(5, 4)
             loop(final, 1, lambda _: true_e(6, 5))
             loop(1 - deep, 1, lambda _: from_below(6, 7))
             with scope("wait_h"):
@@ -481,7 +490,6 @@
             take(h, 1, recv_h, step)
             with later(edges_e(e, 5)):
                 true_e(2, CROSS)
-            loop(final, 1, lambda _: true_e(1, 0))
             loop(1 - deep, 1, lambda _: from_own(0, 0, 0))
 
         with scope("true"):
@@ -498,32 +506,37 @@
     with scope("finish"):
         arrive(send_e, s_sem.at[0])
         arrive(send_h, s_sem.at[1])
-        arrive(raw.at[pl.ds(0, 4)], x_sem.at[0])
+        arrive(raw.at[pl.ds(0, 3)], x_sem.at[3])
         arrive(turned.at[0, :, pl.ds(0, 9 * GHOST)], y_sem.at[GROUPS])
 
     results = [(e, c) for c in range(3)] + [(h, c) for c in range(3)]
     outs = [(e_out, c) for c in range(3)] + [(h_out, c) for c in range(3)]
     with scope("results"):
-        for g in range(2):
-            group = results[4 * g : 4 * g + 4]
-
-            def gather(t):
+        def gather(t):
+            for g in range(2):
+                group = results[4 * g : 4 * g + 4]
                 tiles = [ref[OWN + x, pl.ds(pl.multiple_of(COMP * c + TILE * (t + 1), 8), 8)] for ref, c in group for x in range(4)]
-                tiles = tiles + tiles[: 16 - len(tiles)]
-                whole = jnp.transpose(jnp.concatenate(tiles, 0))
-                for zb in range(8):
+                tiles = jnp.concatenate(tiles, 0)
+                if g == 1:
+                    tiles = jnp.concatenate([tiles, pltpu.roll(tiles, 64, 1)], 0)[:, :64]
+                whole = jnp.transpose(tiles)
+                for zb in range(8 if g == 0 else 4):
                     turned[g, zb, pl.ds(t, 16, stride=10)] = whole[16 * zb : 16 * zb + 16]
 
-            loop_twice(TILES, gather)
-
-            def spread(zb):
-                whole = jnp.transpose(turned[g, zb, pl.ds(16, 128)])
-                for s in range(len(group)):
+        loop_by(2, TILES, gather)
+
+        def spread(g, zb):
+            whole = jnp.transpose(turned[g, zb, pl.ds(16, 128)])
+            group = outs[4 * g : 4 * g + 4]
+            row = 0
+            for block in (zb,) if g == 0 else (zb, zb + 4):
+                for out, c in group:
                     for x in range(4):
-                        out, c = outs[4 * g + s]
-                        out[c, zb, pl.ds(x, 8, stride=4)] = whole[32 * s + 8 * x : 32 * s + 8 * x + 8]
-
-            loop_twice(8, spread)
+                        out[c, block, pl.ds(x, 8, stride=4)] = whole[row : row + 8]
+                        row += 8
+
+        loop(0, 4, lambda zb: (spread(0, 2 * zb), spread(0, 2 * zb + 1), spread(1, zb)))
+
 
 def hand_out(e, h, e_out, h_out, sem):
     copies = [
@@ -561,7 +574,7 @@
             trace, trace, trace, trace,
             pltpu.SemaphoreType.DMA((5,)),
             pltpu.SemaphoreType.DMA((GROUPS + 1,)),
-            pltpu.SemaphoreType.DMA((2,)),
+            pltpu.SemaphoreType.DMA((4,)),
             pltpu.SemaphoreType.DMA((2,)),
             pltpu.SemaphoreType.DMA((8,)),
             pltpu.SemaphoreType.DMA((8,)),

time: 45.2 us -> 44.1 us (0.976)
  Pallas kernels: 44.4 us -> 43.3 us
    pallas_call x1, Pallas kernels: 43.5 us -> 42.4 us  [shards(): pl.pallas_call(kernel, out_shape=(pltpu.VMEM((3, 8, 32, 128), F32),) * 2,...]
where the time goes in v3:
time: 44.1 us; the launch traced here: 44 us
  Pallas kernels  43.3 us (98%)
  between operations  0.64 us (1%)
    pallas_call x1, Pallas kernels, shards(): pl.pallas_call(kernel, out_shape=(pltpu.VMEM((3, 8, 32, 128), F32),) * 2,...  42.4 us
    pallas_call x1, Pallas kernels, shards(): pl.pallas_call(hand_out, out_shape=(jax.ShapeDtypeStruct((3, 8, 32, 128),...  0.93 us

profile of v3, /device:TPU:0, one launch (start us, length us, event | category | flops | bytes accessed | tf_op | source)
XLA Modules:
  0.0 44.0 jit_solution(3130859725747986394)
XLA Ops:
  0.6 42.4 %shard_map.95 = (f32[3,8,32,128]{3,2,1,0:T(8,128)S(1)}, f32[3,8,32,128]{3,2,1,0:T(8,128)S(1)}) custom-call(f32[3,8,32,128]{3,2,1,0:T(8,128)} %bitcast.10, f32[3,8,32,128]{3,2,1,0:T(8,128)} %bitcast.11, f32[3,8,32,128]{3,2,1,0:T(8,128)} %bitcast.12, f32[3,8,32,128]{3,2,1,0:T(8,128)} %bitcast.13, f32[3,8,32,128]{3,2,1,0:T(8,128)} %bitcast.14, ...), custom_call_target="tpu_custom_call" | custom-call | tf_op jit(solution)/shard_map/pallas_call | solution.py:562
  43.1 0.9 %shard_map.96 = (f32[3,8,32,128]{3,2,1,0:T(8,128)}, f32[3,8,32,128]{3,2,1,0:T(8,128)}) custom-call(f32[3,8,32,128]{3,2,1,0:T(8,128)S(1)} %get-tuple-element.6.e, f32[3,8,32,128]{3,2,1,0:T(8,128)S(1)} %get-tuple-element.7.h), custom_call_target="tpu_custom_call" | custom-call | tf_op jit(solution)/shard_map/pallas_call | solution.py:586

commit v4 on v3

--- a/solution.py
+++ b/solution.py
@@ -8,7 +8,7 @@
 from jax.sharding import PartitionSpec as P
 
 STEPS = 14
-BLOCKS = 4
+BLOCKS = 3
 MESH = pl.DeviceIdType.MESH
 NAMED = False
 F32 = jnp.float32
@@ -20,6 +20,7 @@
 OWN = 2
 CROSS = 8
 ZERO_H = 9
+THIRD = 8
 FREE = 10
 ZERO_E = 14
 PLANES = 15
@@ -172,7 +173,7 @@
 
 def kernel(
     e_in, h_in, j_in, p_in, q_in, perm_in, mat_in, abs_in, e_out, h_out,
-    stage, ints, turned, raw, e, h, j, p, q, ah, bh, ae, be, bm,
+    stage, ints, turned, raw, e, h, j, p, q, ah, bh, ae, be, bm, cross,
     send_e, send_h, recv_e, recv_h, in_sem, y_sem, x_sem, s_sem, re_sem, rh_sem,
 ):
     def blank(zb):
@@ -366,11 +367,19 @@
             h_part(OWN, OWN, 0, 0)
             layer(be.at[OWN + 1], be.at[OWN + 5], -1, 2).start()
             layer(be.at[OWN + 2], be.at[OWN - 2], 1, 2).start()
+            ah[OWN + 5] = jnp.zeros((ROWS, 128), F32)
+            for t in range(TILES):
+                here = pl.ds(8 * t, 8)
+                product = be[OWN, here] * bh[OWN, here]
+                for x in range(1, 4):
+                    product = product * (be[OWN + x, here] * bh[OWN + x, here])
+                cross[here] = product
 
     def block(b, carry):
-        size = 3 + b // 2
-        start = 3 * b + b // 3
-        marks = 4 * lax.rem(b, 2) - start
+        size = 4 + (b + 1) // 2
+        start = 4 * b + b // 2
+        far = size // 5
+        marks = 5 * lax.rem(b, 2) - start
 
         def free(i):
             src = OWN + (i // 2) * (FREE - OWN)
@@ -390,14 +399,27 @@
 
         with scope("free"):
             loop(0, size - 1, free)
-            final = start + size - 1
-            give_e(FREE, final, marks + final)
+            end = start + size - 1
             free_h(3, FREE, FREE)
-            give_h(FREE + 3, final, marks + final)
+
+            def give_last(_):
+                give_e(FREE, end, marks + end)
+                give_h(FREE + 3, end, marks + end)
+
+            loop(far, 1, give_last)
+
+            def more_layers(_):
+                for ref in (ae, bm):
+                    layer(ref.at[OWN + 1], ref.at[OWN + 5], -1, 4).start()
+                    layer(ref.at[OWN + 2], ref.at[OWN - 2], 1, 4).start()
+                layer(bh.at[OWN + 1], bh.at[OWN + 5], -1, 4).start()
+                layer(bh.at[OWN + 1], bh.at[THIRD], 1, 4).start()
+
+            loop((b + 3) // 4, 1, more_layers)
 
         with scope("clear"):
             clear((0, 1, 6, 7), (e, h))
-            clear((1, 6), (j, p, q))
+            clear((0, 1, 6, 7), (j, p, q))
 
         def ghost_coefficients(_):
             arrive(raw.at[pl.ds(0, 2)], x_sem.at[0])
@@ -405,10 +427,11 @@
             coefficients(6)
             arrive(raw.at[0, 2], x_sem.at[1])
             coefficients(0, h_alone=True)
+            arrive(be.at[pl.ds(0, 2)], x_sem.at[2])
 
         with scope("ghostcoef"):
             loop((b + 3) // 4, 1, ghost_coefficients)
-            loop(1 - (b // 2) * (1 - b // 3), 1, lambda _: arrive(be.at[pl.ds(0, 2)], x_sem.at[2]))
+            loop(1 - b * (1 - b // 2), 1, lambda _: arrive(be.at[pl.ds(0, 6)], x_sem.at[4]))
 
         def from_own(cell, mag, plane):
             for t in range(TILES):
@@ -440,12 +463,35 @@
 
         with scope("first"):
             answer(send_e, 1, 1, 1)
+            def passed_h(_):
+                trace_h(start, marks + start).wait_recv()
+
+                def give_last(_):
+                    for c in range(2):
+                        for t in range(TILES):
+                            here = pl.ds(8 * t, 8)
+                            below = h[1, at(1 + c, t)] + recv_h[start, c, here]
+                            send_h[end, c, here] = h[FREE + 3, at(1 + c, t)] + cross[here] * below
+                    trace_h(end, marks + end).start()
+
+                loop(1 - far, 1, give_last)
+
+            def passed_e(_):
+                for c in range(2):
+                    for t in range(TILES):
+                        here = pl.ds(8 * t, 8)
+                        send_e[end, c, here] = e[FREE, at(1 + c, t)] + cross[here] * recv_e[start, c, here]
+                trace_e(end, marks + end).start()
+
+            odd = lax.rem(lax.axis_index("gx"), 2)
+            loop(1 - odd, 1, passed_h)
             with scope("wait_e"):
                 trace_e(start, marks + start).wait_recv()
-            answer(recv_e, 5, FREE + 3, 5)
+            loop(1 - far, 1, passed_e)
+            answer(recv_e, 5, FREE + 1, 5)
             from_below(5, 6)
             with scope("wait_h"):
-                trace_h(start, marks + start).wait_recv()
+                loop(odd, 1, passed_h)
             for t in range(TILES):
                 here = pl.ds(8 * t, 8)
                 own = be[2, here]
@@ -455,7 +501,8 @@
         def true(i):
             step = start + i
             final = (i + 1) // size
-            deep = 1 - (i + 2) // size
+            deep = 1 - i // 2
+            wide = far * (i // 2) * (1 - i // 3)
 
             def true_h(x, nxt):
                 h_pass(e, h, ah, bh, x, nxt, x, x)
@@ -463,7 +510,7 @@
             def true_e(x, prv):
                 e_pass(e, h, j, p, q, ae, be, bm, x, x, prv, x, x)
 
-            with later(*(edges_e(e, x) for x in (0, 1, 2, 5, 6))):
+            with later(*(edges_e(e, x) for x in (0, 1, 2, 5, 6, 7))):
                 true_h(3, 4)
                 true_h(4, 5)
             with later(edges_h(h, 3), edges_h(h, 4)):
@@ -480,6 +527,16 @@
             with later(edges_e(e, 3), edges_e(e, 4)):
                 true_h(5, CROSS)
             loop(final, 1, lambda _: true_h(6, 7))
+
+            def wide_h(_):
+                true_h(7, ZERO_E)
+                for t in range(TILES):
+                    b = bh[THIRD, pl.ds(8 * t, 8)]
+                    h[FREE, at(1, t)] = b * e[0, at(2, t)]
+                    h[FREE, at(2, t)] = -b * e[0, at(1, t)]
+                edges_h(h, 7)()
+
+            loop(1 - wide, 1, wide_h)
             for store in (edges_h(h, 5), edges_h(h, 6)):
                 store()
             true_e(5, 4)
@@ -492,13 +549,19 @@
                 true_e(2, CROSS)
             loop(1 - deep, 1, lambda _: from_own(0, 0, 0))
 
+            def wide_e(_):
+                true_e(7, 6)
+                true_e(0, FREE)
+
+            loop(1 - wide, 1, wide_e)
+
         with scope("true"):
             loop(1, size, true)
 
         def onward(_):
-            h_part(OWN, OWN, start + size, 4 * lax.rem(b + 1, 2))
-
-        loop(b // 3, 1, onward)
+            h_part(OWN, OWN, start + size, 5 * lax.rem(b + 1, 2))
+
+        loop(b // 2, 1, onward)
         return carry
 
     lax.fori_loop(0, BLOCKS, block, 0)
@@ -506,7 +569,7 @@
     with scope("finish"):
         arrive(send_e, s_sem.at[0])
         arrive(send_h, s_sem.at[1])
-        arrive(raw.at[pl.ds(0, 3)], x_sem.at[3])
+        arrive(raw.at[pl.ds(0, 5)], x_sem.at[3])
         arrive(turned.at[0, :, pl.ds(0, 9 * GHOST)], y_sem.at[GROUPS])
 
     results = [(e, c) for c in range(3)] + [(h, c) for c in range(3)]
@@ -557,7 +620,7 @@
     cells = [c.reshape(8, 32, 128) for c in (permittivity, material, absorber)]
     wide = pltpu.VMEM((PLANES, 3 * COMP, 128), F32)
     narrow = pltpu.VMEM((PLANES, 3 * ROWS, 128), F32)
-    cell = pltpu.VMEM((8, ROWS, 128), F32)
+    cell = pltpu.VMEM((9, ROWS, 128), F32)
     trace = pltpu.VMEM((STEPS, 2, ROWS, 128), F32)
     e, h = pl.pallas_call(
         kernel,
@@ -570,14 +633,14 @@
             pltpu.VMEM((GROUPS, 8, 160, 128), F32),
             pltpu.VMEM((8, 3, ROWS, 128), F32),
             wide, wide, narrow, narrow, narrow,
-            cell, cell, cell, cell, cell,
+            cell, cell, cell, cell, cell, pltpu.VMEM((ROWS, 128), F32),
             trace, trace, trace, trace,
             pltpu.SemaphoreType.DMA((5,)),
             pltpu.SemaphoreType.DMA((GROUPS + 1,)),
-            pltpu.SemaphoreType.DMA((4,)),
+            pltpu.SemaphoreType.DMA((5,)),
             pltpu.SemaphoreType.DMA((2,)),
-            pltpu.SemaphoreType.DMA((8,)),
-            pltpu.SemaphoreType.DMA((8,)),
+            pltpu.SemaphoreType.DMA((10,)),
+            pltpu.SemaphoreType.DMA((10,)),
         ],
         compiler_params=pltpu.CompilerParams(
             collective_id=0, has_side_effects=True, vmem_limit_bytes=48 * 1024 * 1024

time: 44.1 us -> 41.5 us (0.941)
  Pallas kernels: 43.3 us -> 40.8 us
    pallas_call x1, Pallas kernels: 42.4 us -> 39.8 us  [shards(): pl.pallas_call(kernel, out_shape=(pltpu.VMEM((3, 8, 32, 128), F32),) * 2,...]
where the time goes in v4:
time: 41.5 us; the launch traced here: 41.4 us
  Pallas kernels  40.8 us (98%)
  between operations  0.64 us (2%)
    pallas_call x1, Pallas kernels, shards(): pl.pallas_call(kernel, out_shape=(pltpu.VMEM((3, 8, 32, 128), F32),) * 2,...  39.8 us
    pallas_call x1, Pallas kernels, shards(): pl.pallas_call(hand_out, out_shape=(jax.ShapeDtypeStruct((3, 8, 32, 128),...  0.93 us

profile of v4, /device:TPU:0, one launch (start us, length us, event | category | flops | bytes accessed | tf_op | source)
XLA Modules:
  0.0 41.4 jit_solution(1755632867131295580)
XLA Ops:
  0.6 39.8 %shard_map.95 = (f32[3,8,32,128]{3,2,1,0:T(8,128)S(1)}, f32[3,8,32,128]{3,2,1,0:T(8,128)S(1)}) custom-call(f32[3,8,32,128]{3,2,1,0:T(8,128)} %bitcast.10, f32[3,8,32,128]{3,2,1,0:T(8,128)} %bitcast.11, f32[3,8,32,128]{3,2,1,0:T(8,128)} %bitcast.12, f32[3,8,32,128]{3,2,1,0:T(8,128)} %bitcast.13, f32[3,8,32,128]{3,2,1,0:T(8,128)} %bitcast.14, ...), custom_call_target="tpu_custom_call" | custom-call | tf_op jit(solution)/shard_map/pallas_call | solution.py:625
  40.5 0.9 %shard_map.96 = (f32[3,8,32,128]{3,2,1,0:T(8,128)}, f32[3,8,32,128]{3,2,1,0:T(8,128)}) custom-call(f32[3,8,32,128]{3,2,1,0:T(8,128)S(1)} %get-tuple-element.6.e, f32[3,8,32,128]{3,2,1,0:T(8,128)S(1)} %get-tuple-element.7.h), custom_call_target="tpu_custom_call" | custom-call | tf_op jit(solution)/shard_map/pallas_call | solution.py:649

commit v5 on v4

--- a/solution.py
+++ b/solution.py
@@ -30,7 +30,8 @@
 
 SLOTS = ["perm", "mat", "abs", "e0", "e1", "e2", "h0", "h1", "h2", "j0", "j1", "j2", "p0", "p1", "p2", "q0", "q1", "q2"]
 GROUPS = 5
-GHOST = STEPS
+BELOW = (14, 14, 14, 13, 13)
+ABOVE = (14, 14, 13, 13, 13)
 
 
 def scope(name):
@@ -176,6 +177,15 @@
     stage, ints, turned, raw, e, h, j, p, q, ah, bh, ae, be, bm, cross,
     send_e, send_h, recv_e, recv_h, in_sem, y_sem, x_sem, s_sem, re_sem, rh_sem,
 ):
+    fields = (e_in, h_in, j_in, p_in, q_in)
+    pltpu.make_async_copy(perm_in, stage.at[0], in_sem.at[0]).start()
+    pltpu.make_async_copy(mat_in, ints.at[0], in_sem.at[0]).start()
+    pltpu.make_async_copy(abs_in, ints.at[1], in_sem.at[0]).start()
+    pltpu.make_async_copy(e_in.at[0], stage.at[3], in_sem.at[0]).start()
+    pltpu.make_async_copy(e_in.at[pl.ds(1, 2)], stage.at[pl.ds(4, 2)], in_sem.at[1]).start()
+    for i, f in enumerate(fields[1:], 1):
+        pltpu.make_async_copy(f, stage.at[pl.ds(3 + 3 * i, 3)], in_sem.at[i]).start()
+
     def blank(zb):
         for g in range(GROUPS):
             for edge in (0, 152):
@@ -187,13 +197,6 @@
     for axis in ("gx", "gy"):
         for step in (-1, 1):
             pl.semaphore_signal(barrier, inc=1, device_id=towards(axis, step), device_id_type=MESH)
-
-    fields = (e_in, h_in, j_in, p_in, q_in)
-    pltpu.make_async_copy(perm_in, stage.at[0], in_sem.at[0]).start()
-    pltpu.make_async_copy(mat_in, ints.at[0], in_sem.at[0]).start()
-    pltpu.make_async_copy(abs_in, ints.at[1], in_sem.at[0]).start()
-    for i, f in enumerate(fields):
-        pltpu.make_async_copy(f, stage.at[pl.ds(3 + 3 * i, 3)], in_sem.at[i]).start()
 
     def arrive(ref, sem):
         pltpu.make_async_copy(ref, ref, sem).wait()
@@ -230,7 +233,9 @@
         loop_by(2, 8 if g < 4 else 4, body)
 
     def columns(g, step):
-        source, target = (pl.ds(16, GHOST), pl.ds(144, GHOST)) if step < 0 else (pl.ds(144 - GHOST, GHOST), pl.ds(16 - GHOST, GHOST))
+        count = ABOVE[g] if step < 0 else BELOW[g]
+        source, target = (16, 144) if step < 0 else (144 - count, 16 - count)
+        source, target = pl.ds(source, count), pl.ds(target, count)
         blocks = pl.ds(0, 8 if g < 4 else 4)
         return pltpu.make_async_remote_copy(
             src_ref=turned.at[g, blocks, source], dst_ref=turned.at[g, blocks, target],
@@ -241,7 +246,7 @@
     for g in range(GROUPS):
         with scope("turn"):
             if g < 4:
-                arrive(stage.at[pl.ds(0, 6)] if g == 0 else stage.at[pl.ds(3 + 3 * g, 3)], in_sem.at[g])
+                arrive(stage.at[(pl.ds(0, 4), pl.ds(4, 5), pl.ds(9, 3), pl.ds(12, 3))[g]], in_sem.at[g])
             if g == 3:
                 arrive(stage.at[pl.ds(15, 3)], in_sem.at[4])
             turn(g)
@@ -342,7 +347,6 @@
         trace_h(step, mark).start()
 
     def h_part(src, dst, step, mark):
-        give_e(src, step, mark)
         with later(*(edges_e(e, src + x) for x in range(3))):
             free_h(3, src, dst)
         give_h(dst + 3, step, mark)
@@ -353,7 +357,7 @@
 
     for g in range(GROUPS):
         with scope("ghosts"):
-            arrive(turned.at[g, pl.ds(0, 8 if g < 4 else 4), pl.ds(0, 2 * GHOST)], y_sem.at[g])
+            arrive(turned.at[g, pl.ds(0, 8 if g < 4 else 4), pl.ds(0, BELOW[g] + ABOVE[g])], y_sem.at[g])
         with scope("build"):
             build(g)
         if g == 0:
@@ -364,6 +368,7 @@
         if g == 1:
             loop(OWN, OWN + 4, lambda x: edges_e(e, x)())
         if g == 2:
+            give_e(OWN, 0, 0)
             h_part(OWN, OWN, 0, 0)
             layer(be.at[OWN + 1], be.at[OWN + 5], -1, 2).start()
             layer(be.at[OWN + 2], be.at[OWN - 2], 1, 2).start()
@@ -390,6 +395,7 @@
                 free_e(3, src, dst)
             with later(edges_e(e, dst + 3), edges_h(h, dst + 1), edges_h(h, dst + 2)):
                 free_e(0, src, dst)
+            loop(last * far, 1, lambda _: give_e(dst, start + i + 1, marks + start + i + 1))
 
             def inner(_):
                 free_e(1, src, dst)
@@ -402,11 +408,7 @@
             end = start + size - 1
             free_h(3, FREE, FREE)
 
-            def give_last(_):
-                give_e(FREE, end, marks + end)
-                give_h(FREE + 3, end, marks + end)
-
-            loop(far, 1, give_last)
+            loop(far, 1, lambda _: give_h(FREE + 3, end, marks + end))
 
             def more_layers(_):
                 for ref in (ae, bm):
@@ -427,7 +429,6 @@
             coefficients(6)
             arrive(raw.at[0, 2], x_sem.at[1])
             coefficients(0, h_alone=True)
-            arrive(be.at[pl.ds(0, 2)], x_sem.at[2])
 
         with scope("ghostcoef"):
             loop((b + 3) // 4, 1, ghost_coefficients)
@@ -555,10 +556,14 @@
 
             loop(1 - wide, 1, wide_e)
 
+        with scope("ghostcoef"):
+            loop((b + 3) // 4, 1, lambda _: arrive(be.at[pl.ds(0, 2)], x_sem.at[2]))
+
         with scope("true"):
             loop(1, size, true)
 
         def onward(_):
+            give_e(OWN, start + size, 5 * lax.rem(b + 1, 2))
             h_part(OWN, OWN, start + size, 5 * lax.rem(b + 1, 2))
 
         loop(b // 2, 1, onward)
@@ -570,7 +575,8 @@
         arrive(send_e, s_sem.at[0])
         arrive(send_h, s_sem.at[1])
         arrive(raw.at[pl.ds(0, 5)], x_sem.at[3])
-        arrive(turned.at[0, :, pl.ds(0, 9 * GHOST)], y_sem.at[GROUPS])
+        rows = sum(BELOW[:4]) + sum(ABOVE[:4]) + (BELOW[4] + ABOVE[4]) // 2
+        arrive(turned.at[0, :, pl.ds(0, rows)], y_sem.at[GROUPS])
 
     results = [(e, c) for c in range(3)] + [(h, c) for c in range(3)]
     outs = [(e_out, c) for c in range(3)] + [(h_out, c) for c in range(3)]

time: 41.5 us -> 41.2 us (level)
  no operation moved by 1% of the time
where the time goes in v5:
time: 41.2 us; the launch traced here: 41.1 us
  Pallas kernels  40.5 us (98%)
  between operations  0.64 us (2%)
    pallas_call x1, Pallas kernels, shards(): pl.pallas_call(kernel, out_shape=(pltpu.VMEM((3, 8, 32, 128), F32),) * 2,...  39.5 us
    pallas_call x1, Pallas kernels, shards(): pl.pallas_call(hand_out, out_shape=(jax.ShapeDtypeStruct((3, 8, 32, 128),...  0.93 us

profile of v5, /device:TPU:0, one launch (start us, length us, event | category | flops | bytes accessed | tf_op | source)
XLA Modules:
  0.0 41.1 jit_solution(8394141923826562724)
XLA Ops:
  0.6 39.5 %shard_map.95 = (f32[3,8,32,128]{3,2,1,0:T(8,128)S(1)}, f32[3,8,32,128]{3,2,1,0:T(8,128)S(1)}) custom-call(f32[3,8,32,128]{3,2,1,0:T(8,128)} %bitcast.10, f32[3,8,32,128]{3,2,1,0:T(8,128)} %bitcast.11, f32[3,8,32,128]{3,2,1,0:T(8,128)} %bitcast.12, f32[3,8,32,128]{3,2,1,0:T(8,128)} %bitcast.13, f32[3,8,32,128]{3,2,1,0:T(8,128)} %bitcast.14, ...), custom_call_target="tpu_custom_call" | custom-call | tf_op jit(solution)/shard_map/pallas_call | solution.py:631
  40.2 0.9 %shard_map.96 = (f32[3,8,32,128]{3,2,1,0:T(8,128)}, f32[3,8,32,128]{3,2,1,0:T(8,128)}) custom-call(f32[3,8,32,128]{3,2,1,0:T(8,128)S(1)} %get-tuple-element.6.e, f32[3,8,32,128]{3,2,1,0:T(8,128)S(1)} %get-tuple-element.7.h), custom_call_target="tpu_custom_call" | custom-call | tf_op jit(solution)/shard_map/pallas_call | solution.py:655
